TPU v7x, 32 devices: a whole 2x2x4 slice. The times are simulated.
32 devices in a mesh: groups: 2 (over y), dp: 8 (over z, x), mp: 2 (over core).
Axes of the slice: x: 2, y: 2, z: 4, core: 2. Of those that a mesh axis runs over, the one named last changes fastest.
Arguments:
- inputs: bfloat16 [4096, 4096], P(('groups', 'dp'), 'mp'), parts along dimension 0, may hold values from -36 to 36
- output_gradient_rows: bfloat16 [4096, 14336], P(('groups', 'dp'), 'mp'), parts along dimension 0, may hold values from -144 to 144
- down_adapter_weight: bfloat16 [2, 64, 2048], P('mp', None, 'dp'), may hold values from -0.09375 to 0.09375
- up_adapter_weight: bfloat16 [2, 64, 7168], P('mp', None, 'dp'), may hold values from -0.046875 to 0.046875
- down_gradient_noise: float32 [2, 128, 2048], P('mp', 'groups', 'dp'), parts along dimension 1, may hold values from -5 to 5
- up_gradient_noise: float32 [2, 128, 7168], P('mp', 'groups', 'dp'), parts along dimension 1, may hold values from -5 to 5
Outputs:
- grad_a: float32 [2, 128, 2048], P('mp', 'groups', 'dp'), parts along dimension 1
- grad_b: float32 [2, 128, 7168], P('mp', 'groups', 'dp'), parts along dimension 1
There are 2 independent parts, one for each index of `groups`. A program takes and returns all parts, laid end to end along the dimension named above; an argument that names none is the same for every part. Nothing has to cross between parts.
All inputs are finite; a program needn't handle non-finite values.
Results may differ from a plain program's by a relative error of at most 0.0003.
The roundings to bfloat16 on the way count: a program that leaves them out, or rounds other values in their place, can miss the bound.
Values may be sent and summed in bfloat16 or wider, within the bound.
A program may use at most 64 MiB of HBM per device.

v0:
```python
import math

import jax
import jax.numpy as jnp
from jax import lax
from jax.sharding import PartitionSpec as P

MODEL_WIDTH = 4096
UP_HIDDEN_UNITS = 14336
ADAPTER_RANK = 64
SEQ = 256


clip_ratio = 4.0
noise_ratio = 0.005


def contract_last(left, right):
    return lax.dot_general(
        left, right, (((1,), (1,)), ((), ())), preferred_element_type=jnp.float32
    )


def contract_first(left, right):
    return lax.dot_general(
        left, right, (((0,), (0,)), ((), ())), preferred_element_type=jnp.float32
    )


def per_device(
    inputs,
    output_gradient_rows,
    down_adapter_weight,
    up_adapter_weight,
    down_gradient_noise,
    up_gradient_noise,
):
    clip_bound = clip_ratio * math.sqrt(SEQ * ADAPTER_RANK * (MODEL_WIDTH + UP_HIDDEN_UNITS))
    a_half, b_half = (
        lax.all_gather(down_adapter_weight, "dp", axis=2, tiled=True),
        lax.all_gather(up_adapter_weight, "dp", axis=2, tiled=True),
    )
    u_part = contract_last(inputs, a_half[0])
    v_part = contract_last(output_gradient_rows, b_half[0])
    u_proj, v_proj = lax.psum((u_part, v_part), "mp")
    u_low = u_proj.astype(jnp.bfloat16)
    v_low = v_proj.astype(jnp.bfloat16)
    count = inputs.shape[0] // SEQ
    x_rows = inputs.reshape(count, SEQ, inputs.shape[1])
    g_rows = output_gradient_rows.reshape(count, SEQ, output_gradient_rows.shape[1])
    u_rows = u_low.reshape(count, SEQ, ADAPTER_RANK)
    v_rows = v_low.reshape(count, SEQ, ADAPTER_RANK)
    grad_x = jnp.einsum("esr,esd->erd", v_rows, x_rows, preferred_element_type=jnp.float32)
    grad_g = jnp.einsum("esr,esf->erf", u_rows, g_rows, preferred_element_type=jnp.float32)
    local_sq = jnp.sum(grad_x * grad_x, axis=(1, 2)) + jnp.sum(grad_g * grad_g, axis=(1, 2))
    squares = lax.psum(local_sq, "mp")
    clip_rate = clip_bound / jnp.maximum(jnp.sqrt(squares), clip_bound)
    token_rate = jnp.repeat(clip_rate, SEQ)
    scaled_u = (u_proj * token_rate[:, None]).astype(jnp.bfloat16)
    scaled_v = (v_proj * token_rate[:, None]).astype(jnp.bfloat16)
    part_a = contract_first(scaled_v, inputs)[None]
    part_b = contract_first(scaled_u, output_gradient_rows)[None]
    total_a, total_b = (
        lax.psum_scatter(part_a, "dp", scatter_dimension=2, tiled=True),
        lax.psum_scatter(part_b, "dp", scatter_dimension=2, tiled=True),
    )
    examples = count * lax.axis_size("dp")
    grad_a = (total_a + noise_ratio * clip_bound * down_gradient_noise) / examples
    grad_b = (total_b + noise_ratio * clip_bound * up_gradient_noise) / examples
    return (grad_a, grad_b)


def solution(mesh):
    in_specs = (
        P(("groups", "dp"), "mp"),
        P(("groups", "dp"), "mp"),
        P("mp", None, "dp"),
        P("mp", None, "dp"),
        P("mp", "groups", "dp"),
        P("mp", "groups", "dp"),
    )
    out_specs = (P("mp", "groups", "dp"), P("mp", "groups", "dp"))
    return jax.shard_map(
        per_device, mesh=mesh, in_specs=in_specs, out_specs=out_specs, check_vma=False
    )
```

profile of v0, /device:TPU:0, one launch (start us, length us, event | category | flops | bytes accessed | tf_op | source)
XLA Modules:
  0.0 250.0 jit_solution(12799539300912941462)
XLA Ops:
  7.2 0.0 copy-start
  7.2 0.0 all-reduce.3.cloned.1.call-start
  7.2 32.9 %all_gather.7 = bf16[1,64,2048]{2,1,0:T(8,128)(2,1)S(1)} all-gather(bf16[1,64,256]{2,1,0:T(8,128)(2,1)} %param.8), channel_id=1, replica_groups=mesh['groups'=2,'dp'=8,'mp'=2] {'dp'}, dimensions={2}, use_global_device_ids=true | all-gather | bytes 294912 | tf_op jit(solution)/shard_map/all_gather | solution.py:40
  40.1 32.4 %all_gather.6 = bf16[1,64,7168]{2,1,0:T(8,128)(2,1)S(1)} all-gather(bf16[1,64,896]{2,1,0:T(8,128)(2,1)} %param.9), channel_id=1, replica_groups=mesh['groups'=2,'dp'=8,'mp'=2] {'dp'}, dimensions={2}, use_global_device_ids=true | all-gather | bytes 1032192 | tf_op jit(solution)/shard_map/all_gather | solution.py:41
  72.5 0.0 copy-done
  72.5 1.1 fusion.4
  73.6 3.9 %fusion = f32[256,64]{0,1:T(8,128)} fusion(bf16[256,7168]{1,0:T(8,128)(2,1)} %param.7, bf16[1,64,7168]{2,1,0:T(8,128)(2,1)S(1)} %all_gather.6), kind=kOutput, calls=%fused_computation.4 | convolution fusion | flops 234881024 | bytes 4653056 | tf_op jit(solution)/shard_map/dot_general | solution.py:19
  77.5 0.0 all-reduce.3.cloned.1.call-update
  77.5 0.0 reduce-scatter.3.cloned.1.call-start
  77.6 19.6 %all-reduce.3.cloned.1.call-done = (f32[256,64]{0,1:T(8,128)}, f32[256,64]{0,1:T(8,128)}) async-done(((f32[256,64]{0,1:T(8,128)}, f32[256,64]{0,1:T(8,128)}), (f32[256,64]{0,1:T(8,128)}, f32[256,64]{0,1:T(8,128)})) %all-reduce.3.cloned.1.call-update) | async-done | bytes 131088 | tf_op jit(solution)/shard_map/psum | solution.py:45
  97.2 0.0 copy-start.2
  97.2 0.0 copy-start.1
  97.2 3.5 %fusion.2 = f32[]{:T(128)} fusion(bf16[256,7168]{1,0:T(8,128)(2,1)} %param.7, f32[256,64]{0,1:T(8,128)} %get-tuple-element.3), kind=kOutput, calls=%fused_computation.6 | convolution fusion | flops 235814912 | bytes 3735556 | tf_op jit(solution)/shard_map/esr,esf->erf/dot_general | solution.py:54
  100.7 0.0 copy-done.2
  100.7 0.9 fusion.3
  102.9 3.6 %psum.23 = f32[1]{0:T(128)} all-reduce(f32[1]{0:T(128)} %bitcast.2), channel_id=1, replica_groups=mesh['groups'=2,'dp'=8,'mp'=2] {'mp'}, use_global_device_ids=true, to_apply=%region_4.0 | all-reduce | flops 1 | bytes 8 | tf_op jit(solution)/shard_map/psum | solution.py:56
  107.2 1.1 convolution_bitcast_fusion.1
  108.3 0.0 reduce-scatter.3.cloned.1.call-update
  108.3 0.0 copy-start.4
  108.4 0.0 copy-start.3
  108.4 0.0 reduce-scatter.5.cloned.1.call-start
  108.4 0.0 copy-done.1
  108.4 4.1 %convolution_bitcast_fusion = f32[1,64,7168]{2,1,0:T(8,128)} fusion(bf16[256,7168]{1,0:T(8,128)(2,1)} %param.7, f32[256,64]{0,1:T(8,128)S(1)} %copy-done.1, f32[]{:T(128)} %bitcast.3), kind=kOutput, calls=%fused_computation.1 | convolution fusion | flops 234913792 | bytes 5570564 | tf_op jit(solution)/shard_map/dot_general | solution.py:25
  112.5 0.0 reduce-scatter.5.cloned.1.call-update
  112.6 59.5 %reduce-scatter.3.cloned.1.call-done = f32[1,64,256]{2,1,0:T(8,128)} async-done(((f32[1,64,2048]{2,1,0:T(8,128)}), f32[1,64,256]{2,1,0:T(8,128)}) %reduce-scatter.3.cloned.1.call-update) | async-done | bytes 65552 | tf_op jit(solution)/shard_map/reduce_scatter | solution.py:64
  172.0 0.0 copy-done.4
  172.0 1.5 add_multiply_fusion.1
  173.5 68.2 %reduce-scatter.5.cloned.1.call-done = f32[1,64,896]{2,1,0:T(8,128)} async-done(((f32[1,64,7168]{2,1,0:T(8,128)}), f32[1,64,896]{2,1,0:T(8,128)}) %reduce-scatter.5.cloned.1.call-update) | async-done | bytes 229392 | tf_op jit(solution)/shard_map/reduce_scatter | solution.py:65
  241.8 0.0 copy-done.3
  241.8 1.7 add_multiply_fusion
Async XLA Ops:
  7.2 65.3 %copy-start = (bf16[256,2048]{1,0:T(8,128)(2,1)S(1)}, bf16[256,2048]{1,0:T(8,128)(2,1)}, u32[]{:S(2)}) copy-start(bf16[256,2048]{1,0:T(8,128)(2,1)} %param.6) | copy-start | bytes 3145732
  7.2 90.0 %all-reduce.3.cloned.1.call-start = ((), (), s32[]{:S(2)}) async-start(), calls=%async_computation.4 | async-start | bytes 262144 | tf_op jit(solution)/shard_map/psum | solution.py:45
  77.5 94.5 %reduce-scatter.3.cloned.1.call-start = ((), (), s32[]{:S(2)}) async-start(), calls=%async_computation.2 | async-start | bytes 589824 | tf_op jit(solution)/shard_map/reduce_scatter | solution.py:64
  97.2 3.5 %copy-start.2 = (f32[256,64]{0,1:T(8,128)S(1)}, f32[256,64]{0,1:T(8,128)}, u32[]{:S(2)}) copy-start(f32[256,64]{0,1:T(8,128)} %get-tuple-element.2) | copy-start | bytes 196612
  97.2 11.3 %copy-start.1 = (f32[256,64]{0,1:T(8,128)S(1)}, f32[256,64]{0,1:T(8,128)}, u32[]{:S(2)}) copy-start(f32[256,64]{0,1:T(8,128)} %get-tuple-element.3) | copy-start | bytes 196612
  108.3 63.7 %copy-start.4 = (f32[1,64,256]{2,1,0:T(8,128)S(1)}, f32[1,64,256]{2,1,0:T(8,128)}, u32[]{:S(2)}) copy-start(f32[1,64,256]{2,1,0:T(8,128)} %param.10) | copy-start | bytes 196612
  108.4 133.4 %copy-start.3 = (f32[1,64,896]{2,1,0:T(8,128)S(1)}, f32[1,64,896]{2,1,0:T(8,128)}, u32[]{:S(2)}) copy-start(f32[1,64,896]{2,1,0:T(8,128)} %param.11) | copy-start | bytes 688132
  108.4 133.4 %reduce-scatter.5.cloned.1.call-start = ((), (), s32[]{:S(2)}) async-start(), calls=%async_computation.3 | async-start | bytes 2064384 | tf_op jit(solution)/shard_map/reduce_scatter | solution.py:65
Sparse Core Ops, SparseCore 0:
  77.6 19.4 all-reduce.2
  108.5 63.5 reduce-scatter.2
  175.9 65.8 reduce-scatter.4
where the time goes:
time: 250 us
  waiting for transfers between devices  147 us (59%)
  blocking collectives  68.9 us (28%)
  between operations  15.8 us (6%)
  matrix products  14.6 us (6%)
  other arithmetic  3.14 us (1%)
    reduce_scatter x1, waiting for transfers between devices, per_device(): lax.psum_scatter(part_b, 'dp', scatter_dimension=2, tiled=True)  68.2 us
    reduce_scatter x1, waiting for transfers between devices, per_device(): lax.psum_scatter(part_a, 'dp', scatter_dimension=2, tiled=True)  59.5 us
    all_gather x1, blocking collectives, per_device(): lax.all_gather(down_adapter_weight, 'dp', axis=2, tiled=True)  32.9 us
    all_gather x1, blocking collectives, per_device(): lax.all_gather(up_adapter_weight, 'dp', axis=2, tiled=True)  32.4 us
    psum x1, waiting for transfers between devices, per_device(): u_proj, v_proj = lax.psum((u_part, v_part), 'mp')  19.6 us
    dot_general x2, matrix products, contract_first(): lax.dot_general(left, right, (((0,), (0,)), ((), ())), preferred_element_...  5.22 us
  transfers between devices with their start and end apart: 3, of which 3 were waited for; matrix products, arithmetic and copies ran while one was open for 2% of the time, Pallas kernels for 0%

commit v1 on v0

--- a/solution.py
+++ b/solution.py
@@ -1,8 +1,11 @@
+import functools
 import math
 
 import jax
 import jax.numpy as jnp
 from jax import lax
+from jax.experimental import pallas as pl
+from jax.experimental.pallas import tpu as pltpu
 from jax.sharding import PartitionSpec as P
 
 MODEL_WIDTH = 4096
@@ -10,9 +13,11 @@
 ADAPTER_RANK = 64
 SEQ = 256
 
+INNER = 2
 
 clip_ratio = 4.0
 noise_ratio = 0.005
+clip_bound = clip_ratio * math.sqrt(SEQ * ADAPTER_RANK * (MODEL_WIDTH + UP_HIDDEN_UNITS))
 
 
 def contract_last(left, right):
@@ -35,7 +40,6 @@
     down_gradient_noise,
     up_gradient_noise,
 ):
-    clip_bound = clip_ratio * math.sqrt(SEQ * ADAPTER_RANK * (MODEL_WIDTH + UP_HIDDEN_UNITS))
     a_half, b_half = (
         lax.all_gather(down_adapter_weight, "dp", axis=2, tiled=True),
         lax.all_gather(up_adapter_weight, "dp", axis=2, tiled=True),
@@ -70,6 +74,304 @@
     return (grad_a, grad_b)
 
 
+def send(src, dst, send_sem, recv_sem, axis, index):
+    copy = pltpu.make_async_remote_copy(
+        src_ref=src,
+        dst_ref=dst,
+        send_sem=send_sem,
+        recv_sem=recv_sem,
+        device_id={axis: index},
+        device_id_type=pl.DeviceIdType.MESH,
+    )
+    copy.start()
+    return copy
+
+
+def arrived(dst, send_sem, recv_sem, axis, index):
+    pltpu.make_async_remote_copy(
+        src_ref=dst,
+        dst_ref=dst,
+        send_sem=send_sem,
+        recv_sem=recv_sem,
+        device_id={axis: index},
+        device_id_type=pl.DeviceIdType.MESH,
+    ).wait_recv()
+
+
+def target_order(depth):
+    order = []
+    for step in range((depth + 1) // 2):
+        order.append(depth - 1 - step)
+        if step != depth - 1 - step:
+            order.append(step)
+    return order
+
+
+def kernel(
+    depth,
+    x_ref, g_ref, a_ref, b_ref, noise_a_ref, noise_b_ref,
+    out_a_ref, out_b_ref,
+    x_rows, g_rows, a_all, b_all, noise_a, noise_b,
+    uv_mine, uv_other, sq_mine, sq_other,
+    cross_out, cross_in, held, up_in, down_in,
+    local_sem, gather_send, gather_recv, pair_send, pair_recv,
+    cross_send, cross_recv, up_send, up_recv, down_send, down_recv,
+):
+    dp = lax.axis_index("dp")
+    mp = lax.axis_index("mp")
+    z = dp // INNER
+    x = dp % INNER
+    other_x = 1 - x
+    across = z * INNER + other_x
+    rank = a_ref.shape[1]
+    wa = a_ref.shape[2]
+    wb = b_ref.shape[2]
+    examples = depth * INNER
+
+    def local(src, dst, index):
+        copy = pltpu.make_async_copy(src, dst, local_sem.at[index])
+        copy.start()
+        return copy
+
+    own_a = local(a_ref.at[0], a_all.at[dp], 0)
+    own_b = local(b_ref.at[0], b_all.at[dp], 1)
+    load_x = local(x_ref, x_rows, 2)
+    load_g = local(g_ref, g_rows, 3)
+    load_na = local(noise_a_ref.at[0], noise_a, 4)
+    load_nb = local(noise_b_ref.at[0], noise_b, 5)
+
+    peers = [lax.rem(z + d, depth) for d in range(1, depth)]
+    barrier = pltpu.get_barrier_semaphore()
+    for axis, index in [("dp", across), ("mp", 1 - mp)] + [
+        ("dp", p * INNER + x) for p in peers
+    ]:
+        pl.semaphore_signal(
+            barrier, inc=1, device_id={axis: index}, device_id_type=pl.DeviceIdType.MESH
+        )
+    pl.semaphore_wait(barrier, 2 + len(peers))
+
+    copies = []
+    own_a.wait()
+    own_b.wait()
+
+    def give(slot, count, index):
+        for which, whole in ((0, a_all), (1, b_all)):
+            copies.append(
+                send(
+                    whole.at[slot], whole.at[slot],
+                    gather_send.at[which, count], gather_recv.at[which, slot],
+                    "dp", index,
+                )
+            )
+
+    def take(slot):
+        for which, whole in ((0, a_all), (1, b_all)):
+            arrived(whole.at[slot], gather_send.at[which, 0], gather_recv.at[which, slot], "dp", across)
+
+    give(dp, 0, across)
+    for number, p in enumerate(peers):
+        give(dp, 1 + number, p * INNER + x)
+
+    def project(slot):
+        u = contract_last(a_all[slot], x_rows[:, pl.ds(pl.multiple_of(slot * wa, 128), wa)])
+        v = contract_last(b_all[slot], g_rows[:, pl.ds(pl.multiple_of(slot * wb, 128), wb)])
+        return u, v
+
+    load_x.wait()
+    load_g.wait()
+    u, v = project(dp)
+    for number, p in enumerate(peers):
+        slot = p * INNER + x
+        take(slot)
+        give(slot, depth + number, across)
+        more = project(slot)
+        u, v = u + more[0], v + more[1]
+    for p in [z] + peers:
+        slot = p * INNER + other_x
+        take(slot)
+        more = project(slot)
+        u, v = u + more[0], v + more[1]
+
+    uv_mine[0] = u
+    uv_mine[1] = v
+    copy = send(uv_mine, uv_other, pair_send.at[0], pair_recv.at[0], "mp", 1 - mp)
+    copy.wait()
+    u = u + uv_other[0]
+    v = v + uv_other[1]
+    u_low = u.astype(jnp.bfloat16)
+    v_low = v.astype(jnp.bfloat16)
+
+    def product(low, rows, block, width):
+        return jnp.dot(
+            low, rows[:, block * width:(block + 1) * width], preferred_element_type=jnp.float32
+        )
+
+    sq_a = jnp.zeros((1, wa), jnp.float32)
+    sq_b = jnp.zeros((1, wb), jnp.float32)
+    for block in range(examples):
+        part = product(v_low, x_rows, block, wa)
+        sq_a = sq_a + jnp.sum(part * part, axis=0, keepdims=True)
+        part = product(u_low, g_rows, block, wb)
+        sq_b = sq_b + jnp.sum(part * part, axis=0, keepdims=True)
+    sq = jnp.sum(sq_a, axis=1, keepdims=True) + jnp.sum(sq_b, axis=1, keepdims=True)
+    sq_mine[...] = jnp.broadcast_to(sq, sq_mine.shape)
+    copy = send(sq_mine, sq_other, pair_send.at[1], pair_recv.at[1], "mp", 1 - mp)
+    copy.wait()
+    squares = sq_mine[...] + sq_other[...]
+    rate = (clip_bound / jnp.maximum(jnp.sqrt(squares), clip_bound))[0:1, 0:1]
+    u_scaled = (u * rate).astype(jnp.bfloat16)
+    v_scaled = (v * rate).astype(jnp.bfloat16)
+
+    def piece(target, side):
+        slot = target * INNER + side
+        part_a = jnp.dot(
+            v_scaled, x_rows[:, pl.ds(pl.multiple_of(slot * wa, 128), wa)],
+            preferred_element_type=jnp.float32,
+        )
+        part_b = jnp.dot(
+            u_scaled, g_rows[:, pl.ds(pl.multiple_of(slot * wb, 128), wb)],
+            preferred_element_type=jnp.float32,
+        )
+        return part_a, part_b
+
+    order = target_order(depth)
+    for target in order:
+        part_a, part_b = piece(target, other_x)
+        cross_out[target, :, :wa] = part_a
+        cross_out[target, :, wa:] = part_b
+        copies.append(
+            send(
+                cross_out.at[target], cross_in.at[target],
+                cross_send.at[target], cross_recv.at[target], "dp", across,
+            )
+        )
+    for target in order:
+        part_a, part_b = piece(target, x)
+        held[target, :, :wa] = part_a
+        held[target, :, wa:] = part_b
+
+    above = dp + INNER
+    below = dp - INNER
+
+    def from_below(target):
+        arrived(up_in.at[target], up_send.at[target], up_recv.at[target], "dp", dp)
+        held[target] = held[target] + up_in[target]
+
+    def from_above(target):
+        arrived(down_in.at[target], down_send.at[target], down_recv.at[target], "dp", dp)
+        held[target] = held[target] + down_in[target]
+
+    for target in order:
+        arrived(cross_in.at[target], cross_send.at[target], cross_recv.at[target], "dp", across)
+        held[target] = held[target] + cross_in[target]
+
+        @pl.when(z < target)
+        def _():
+            @pl.when(z > 0)
+            def _():
+                from_below(target)
+
+            send(held.at[target], up_in.at[target], up_send.at[target], up_recv.at[target], "dp", above)
+
+        @pl.when(z > target)
+        def _():
+            @pl.when(z < depth - 1)
+            def _():
+                from_above(target)
+
+            send(
+                held.at[target], down_in.at[target],
+                down_send.at[target], down_recv.at[target], "dp", below,
+            )
+
+    load_na.wait()
+    load_nb.wait()
+    scale = noise_ratio * clip_bound
+    for target in range(depth):
+
+        @pl.when(z == target)
+        def _():
+            if target > 0:
+                from_below(target)
+            if target < depth - 1:
+                from_above(target)
+            out_a_ref[0] = (held[target, :, :wa] + scale * noise_a[...]) / examples
+            out_b_ref[0] = (held[target, :, wa:] + scale * noise_b[...]) / examples
+
+    for copy in copies:
+        copy.wait_send()
+    for target in range(depth):
+
+        @pl.when(z < target)
+        def _():
+            pltpu.make_async_remote_copy(
+                src_ref=held.at[target], dst_ref=up_in.at[target],
+                send_sem=up_send.at[target], recv_sem=up_recv.at[target],
+                device_id={"dp": above}, device_id_type=pl.DeviceIdType.MESH,
+            ).wait_send()
+
+        @pl.when(z > target)
+        def _():
+            pltpu.make_async_remote_copy(
+                src_ref=held.at[target], dst_ref=down_in.at[target],
+                send_sem=down_send.at[target], recv_sem=down_recv.at[target],
+                device_id={"dp": below}, device_id_type=pl.DeviceIdType.MESH,
+            ).wait_send()
+
+
+def fused(depth, inputs, rows, down, up, noise_a, noise_b):
+    rank, wa = down.shape[1:]
+    wb = up.shape[2]
+    dp = depth * INNER
+    f32, bf16 = jnp.float32, jnp.bfloat16
+    dma = pltpu.SemaphoreType.DMA
+    return pl.pallas_call(
+        functools.partial(kernel, depth),
+        out_shape=(
+            jax.ShapeDtypeStruct(noise_a.shape, f32),
+            jax.ShapeDtypeStruct(noise_b.shape, f32),
+        ),
+        in_specs=[pl.BlockSpec(memory_space=pl.ANY)] * 6,
+        out_specs=(pl.BlockSpec(memory_space=pltpu.VMEM), pl.BlockSpec(memory_space=pltpu.VMEM)),
+        scratch_shapes=[
+            pltpu.VMEM(inputs.shape, bf16),
+            pltpu.VMEM(rows.shape, bf16),
+            pltpu.VMEM((dp, rank, wa), bf16),
+            pltpu.VMEM((dp, rank, wb), bf16),
+            pltpu.VMEM((rank, wa), f32),
+            pltpu.VMEM((rank, wb), f32),
+            pltpu.VMEM((2, rank, SEQ), f32),
+            pltpu.VMEM((2, rank, SEQ), f32),
+            pltpu.VMEM((8, 128), f32),
+            pltpu.VMEM((8, 128), f32),
+            pltpu.VMEM((depth, rank, wa + wb), f32),
+            pltpu.VMEM((depth, rank, wa + wb), f32),
+            pltpu.VMEM((depth, rank, wa + wb), f32),
+            pltpu.VMEM((depth, rank, wa + wb), f32),
+            pltpu.VMEM((depth, rank, wa + wb), f32),
+            dma((6,)),
+            dma((2, 2 * depth)),
+            dma((2, dp)),
+            dma((2,)),
+            dma((2,)),
+            dma((depth,)),
+            dma((depth,)),
+            dma((depth,)),
+            dma((depth,)),
+            dma((depth,)),
+            dma((depth,)),
+        ],
+        compiler_params=pltpu.CompilerParams(
+            collective_id=0, has_side_effects=True, vmem_limit_bytes=40 * 1024 * 1024
+        ),
+        cost_estimate=pl.CostEstimate(
+            flops=6 * rank * SEQ * dp * (wa + wb),
+            bytes_accessed=2 * SEQ * dp * (wa + wb),
+            transcendentals=0,
+        ),
+    )(inputs, rows, down, up, noise_a, noise_b)
+
+
 def solution(mesh):
     in_specs = (
         P(("groups", "dp"), "mp"),
@@ -80,6 +382,21 @@
         P("mp", "groups", "dp"),
     )
     out_specs = (P("mp", "groups", "dp"), P("mp", "groups", "dp"))
+    devices = mesh.shape["dp"]
+
+    def body(inputs, rows, down, up, noise_a, noise_b):
+        fits = (
+            devices % INNER == 0
+            and 4 <= devices <= 16
+            and mesh.shape["mp"] == 2
+            and inputs.shape[0] == SEQ
+            and down.shape[2] % 128 == 0
+            and up.shape[2] % 128 == 0
+        )
+        if fits:
+            return fused(devices // INNER, inputs, rows, down, up, noise_a, noise_b)
+        return per_device(inputs, rows, down, up, noise_a, noise_b)
+
     return jax.shard_map(
-        per_device, mesh=mesh, in_specs=in_specs, out_specs=out_specs, check_vma=False
-    )
+        body, mesh=mesh, in_specs=in_specs, out_specs=out_specs, check_vma=False
+    )

time: 250 us -> 82.7 us (0.33)
  the two profiles are of different devices: /device:TPU:0 before, /device:TPU:8 now
where the time goes in v1:
time: 82.7 us; the launch traced here: 82.4 us
  Pallas kernels  73.7 us (89%)
  local copies, waits for them, and re-layouts  8.01 us (10%)
    pallas_call x1, Pallas kernels, fused(): pl.pallas_call(functools.partial(kernel, depth), out_shape=(jax.ShapeDtyp...  73.7 us
    unnamed x14, local copies, waits for them, and re-layouts  8.01 us

profile of v1, /device:TPU:8, one launch (start us, length us, event | category | flops | bytes accessed | tf_op | source)
XLA Modules:
  0.0 82.4 jit_solution(13072584204060865238)
XLA Ops:
  0.6 0.0 copy-start
  0.6 2.0 %copy-done = bf16[256,7168]{1,0:T(8,128)(2,1)S(1)} copy-done((bf16[256,7168]{1,0:T(8,128)(2,1)S(1)}, bf16[256,7168]{1,0:T(8,128)(2,1)}, u32[]{:S(2)}) %copy-start) | copy-done | bytes 3670040
  2.7 0.0 copy-start.1
  2.7 1.2 %copy-done.1 = bf16[256,2048]{1,0:T(8,128)(2,1)S(1)} copy-done((bf16[256,2048]{1,0:T(8,128)(2,1)S(1)}, bf16[256,2048]{1,0:T(8,128)(2,1)}, u32[]{:S(2)}) %copy-start.1) | copy-done | bytes 1048600
  3.9 0.0 copy-start.2
  3.9 0.9 %copy-done.2 = f32[1,64,896]{2,1,0:T(8,128)S(1)} copy-done((f32[1,64,896]{2,1,0:T(8,128)S(1)}, f32[1,64,896]{2,1,0:T(8,128)}, u32[]{:S(2)}) %copy-start.2) | copy-done | bytes 229400
  4.8 0.0 copy-start.3
  4.8 0.9 %copy-done.3 = bf16[1,64,896]{2,1,0:T(8,128)(2,1)S(1)} copy-done((bf16[1,64,896]{2,1,0:T(8,128)(2,1)S(1)}, bf16[1,64,896]{2,1,0:T(8,128)(2,1)}, u32[]{:S(2)}) %copy-start.3) | copy-done | bytes 114712
  5.7 0.0 copy-start.4
  5.7 0.8 %copy-done.4 = f32[1,64,256]{2,1,0:T(8,128)S(1)} copy-done((f32[1,64,256]{2,1,0:T(8,128)S(1)}, f32[1,64,256]{2,1,0:T(8,128)}, u32[]{:S(2)}) %copy-start.4) | copy-done | bytes 65560
  6.6 0.0 copy-start.5
  6.6 0.8 copy-done.5
  7.3 73.7 %shard_map.77 = (f32[1,64,256]{2,1,0:T(8,128)S(1)}, f32[1,64,896]{2,1,0:T(8,128)S(1)}) custom-call(bf16[256,2048]{1,0:T(8,128)(2,1)S(1)} %copy-done.1, bf16[256,7168]{1,0:T(8,128)(2,1)S(1)} %copy-done, bf16[1,64,256]{2,1,0:T(8,128)(2,1)S(1)} %copy-done.5, bf16[1,64,896]{2,1,0:T(8,128)(2,1)S(1)} %copy-done.3, f32[1,64,256]{2,1,0:T(8,128)S(1)} %copy-done.4, ...), custom_call_target="tpu_custom_call" | custom-call | flops 905969664 | bytes 4718592 | tf_op jit(solution)/shard_map/pallas_call | solution.py:328
  81.1 0.6 copy.10
  81.7 0.7 copy.11
Async XLA Ops:
  0.6 2.0 %copy-start = (bf16[256,7168]{1,0:T(8,128)(2,1)S(1)}, bf16[256,7168]{1,0:T(8,128)(2,1)}, u32[]{:S(2)}) copy-start(bf16[256,7168]{1,0:T(8,128)(2,1)} %g_ref.1) | copy-start | bytes 11010052
  2.7 1.2 %copy-start.1 = (bf16[256,2048]{1,0:T(8,128)(2,1)S(1)}, bf16[256,2048]{1,0:T(8,128)(2,1)}, u32[]{:S(2)}) copy-start(bf16[256,2048]{1,0:T(8,128)(2,1)} %x_ref.1) | copy-start | bytes 3145732
  3.9 0.9 %copy-start.2 = (f32[1,64,896]{2,1,0:T(8,128)S(1)}, f32[1,64,896]{2,1,0:T(8,128)}, u32[]{:S(2)}) copy-start(f32[1,64,896]{2,1,0:T(8,128)} %noise_b_ref.1) | copy-start | bytes 688132
  4.8 0.9 %copy-start.3 = (bf16[1,64,896]{2,1,0:T(8,128)(2,1)S(1)}, bf16[1,64,896]{2,1,0:T(8,128)(2,1)}, u32[]{:S(2)}) copy-start(bf16[1,64,896]{2,1,0:T(8,128)(2,1)} %b_ref.1) | copy-start | bytes 344068
  5.7 0.8 %copy-start.4 = (f32[1,64,256]{2,1,0:T(8,128)S(1)}, f32[1,64,256]{2,1,0:T(8,128)}, u32[]{:S(2)}) copy-start(f32[1,64,256]{2,1,0:T(8,128)} %noise_a_ref.1) | copy-start | bytes 196612
  6.6 0.8 copy-start.5

commit v2 on v1

--- a/solution.py
+++ b/solution.py
@@ -14,6 +14,8 @@
 SEQ = 256
 
 INNER = 2
+GATHER_CUTS = 2
+REDUCE_CUTS = 2
 
 clip_ratio = 4.0
 noise_ratio = 0.005
@@ -74,8 +76,8 @@
     return (grad_a, grad_b)
 
 
-def send(src, dst, send_sem, recv_sem, axis, index):
-    copy = pltpu.make_async_remote_copy(
+def remote(src, dst, send_sem, recv_sem, axis, index):
+    return pltpu.make_async_remote_copy(
         src_ref=src,
         dst_ref=dst,
         send_sem=send_sem,
@@ -83,28 +85,26 @@
         device_id={axis: index},
         device_id_type=pl.DeviceIdType.MESH,
     )
-    copy.start()
-    return copy
-
-
-def arrived(dst, send_sem, recv_sem, axis, index):
-    pltpu.make_async_remote_copy(
-        src_ref=dst,
-        dst_ref=dst,
-        send_sem=send_sem,
-        recv_sem=recv_sem,
-        device_id={axis: index},
-        device_id_type=pl.DeviceIdType.MESH,
-    ).wait_recv()
-
-
-def target_order(depth):
-    order = []
-    for step in range((depth + 1) // 2):
-        order.append(depth - 1 - step)
-        if step != depth - 1 - step:
-            order.append(step)
-    return order
+
+
+def gather_order(depth):
+    return [sorted((p for p in range(depth) if p != z), key=lambda p: abs(p - z)) for z in range(depth)]
+
+
+def reduce_order(depth):
+    table = []
+    for z in range(depth):
+        up = list(range(depth - 1, z, -1))
+        down = list(range(z))
+        table.append((up + down if len(up) >= len(down) else down + up) + [z])
+    return table
+
+
+def pick(table, step, z):
+    entry = jnp.int32(table[0][step])
+    for row in range(1, len(table)):
+        entry = jnp.where(z == row, jnp.int32(table[row][step]), entry)
+    return entry
 
 
 def kernel(
@@ -123,10 +123,14 @@
     x = dp % INNER
     other_x = 1 - x
     across = z * INNER + other_x
+    above = dp + INNER
+    below = dp - INNER
     rank = a_ref.shape[1]
     wa = a_ref.shape[2]
     wb = b_ref.shape[2]
     examples = depth * INNER
+    has_above = z < depth - 1
+    has_below = z > 0
 
     def local(src, dst, index):
         copy = pltpu.make_async_copy(src, dst, local_sem.at[index])
@@ -140,61 +144,112 @@
     load_na = local(noise_a_ref.at[0], noise_a, 4)
     load_nb = local(noise_b_ref.at[0], noise_b, 5)
 
-    peers = [lax.rem(z + d, depth) for d in range(1, depth)]
     barrier = pltpu.get_barrier_semaphore()
-    for axis, index in [("dp", across), ("mp", 1 - mp)] + [
-        ("dp", p * INNER + x) for p in peers
-    ]:
+
+    def greet(axis, index):
         pl.semaphore_signal(
             barrier, inc=1, device_id={axis: index}, device_id_type=pl.DeviceIdType.MESH
         )
-    pl.semaphore_wait(barrier, 2 + len(peers))
-
-    copies = []
+
+    greet("dp", across)
+    greet("mp", 1 - mp)
+
+    @pl.when(has_above)
+    def _():
+        greet("dp", above)
+
+    @pl.when(has_below)
+    def _():
+        greet("dp", below)
+
+    @pl.when(has_above & has_below)
+    def _():
+        pl.semaphore_wait(barrier, 4)
+
+    @pl.when(jnp.logical_not(has_above & has_below))
+    def _():
+        pl.semaphore_wait(barrier, 3)
+
     own_a.wait()
     own_b.wait()
 
-    def give(slot, count, index):
-        for which, whole in ((0, a_all), (1, b_all)):
-            copies.append(
-                send(
-                    whole.at[slot], whole.at[slot],
-                    gather_send.at[which, count], gather_recv.at[which, slot],
-                    "dp", index,
-                )
-            )
-
-    def take(slot):
-        for which, whole in ((0, a_all), (1, b_all)):
-            arrived(whole.at[slot], gather_send.at[which, 0], gather_recv.at[which, slot], "dp", across)
-
-    give(dp, 0, across)
-    for number, p in enumerate(peers):
-        give(dp, 1 + number, p * INNER + x)
+    def chunk(which, cut):
+        size = rank // GATHER_CUTS
+        return ((a_all, b_all)[which]), pl.ds(cut * size, size)
+
+    parts = [(which, cut) for cut in range(GATHER_CUTS) for which in (0, 1)]
+
+    def give(part, row, way, index):
+        which, cut = part
+        whole, rows = chunk(which, cut)
+        slot = row * INNER + x
+        return remote(
+            whole.at[slot, rows], whole.at[slot, rows],
+            gather_send.at[way, which, cut, row], gather_recv.at[which, cut, slot],
+            "dp", index,
+        )
+
+    def take(part, slot):
+        which, cut = part
+        whole, rows = chunk(which, cut)
+        remote(
+            whole.at[slot, rows], whole.at[slot, rows],
+            gather_send.at[0, which, cut, 0], gather_recv.at[which, cut, slot],
+            "dp", across,
+        ).wait_recv()
+
+    def pass_on(part, row, act):
+        @pl.when(has_above & (row <= z))
+        def _():
+            act(give(part, row, 1, above))
+
+        @pl.when(has_below & (row >= z))
+        def _():
+            act(give(part, row, 2, below))
+
+        act(give(part, row, 0, across))
+
+    def start(copy):
+        copy.start()
+
+    def finish(copy):
+        copy.wait_send()
 
     def project(slot):
         u = contract_last(a_all[slot], x_rows[:, pl.ds(pl.multiple_of(slot * wa, 128), wa)])
         v = contract_last(b_all[slot], g_rows[:, pl.ds(pl.multiple_of(slot * wb, 128), wb)])
         return u, v
 
+    for part in parts:
+        pass_on(part, z, start)
+    near = gather_order(depth)
+    rows_of = [pick(near, step, z) for step in range(depth - 1)]
     load_x.wait()
     load_g.wait()
     u, v = project(dp)
-    for number, p in enumerate(peers):
-        slot = p * INNER + x
-        take(slot)
-        give(slot, depth + number, across)
+
+    def take_across(row, u, v):
+        slot = row * INNER + other_x
+        for part in parts:
+            take(part, slot)
         more = project(slot)
+        return u + more[0], v + more[1]
+
+    last = z
+    for row in rows_of:
+        for part in parts:
+            take(part, row * INNER + x)
+            pass_on(part, row, start)
+        more = project(row * INNER + x)
         u, v = u + more[0], v + more[1]
-    for p in [z] + peers:
-        slot = p * INNER + other_x
-        take(slot)
-        more = project(slot)
-        u, v = u + more[0], v + more[1]
+        u, v = take_across(last, u, v)
+        last = row
+    u, v = take_across(last, u, v)
 
     uv_mine[0] = u
     uv_mine[1] = v
-    copy = send(uv_mine, uv_other, pair_send.at[0], pair_recv.at[0], "mp", 1 - mp)
+    copy = remote(uv_mine, uv_other, pair_send.at[0], pair_recv.at[0], "mp", 1 - mp)
+    copy.start()
     copy.wait()
     u = u + uv_other[0]
     v = v + uv_other[1]
@@ -215,7 +270,8 @@
         sq_b = sq_b + jnp.sum(part * part, axis=0, keepdims=True)
     sq = jnp.sum(sq_a, axis=1, keepdims=True) + jnp.sum(sq_b, axis=1, keepdims=True)
     sq_mine[...] = jnp.broadcast_to(sq, sq_mine.shape)
-    copy = send(sq_mine, sq_other, pair_send.at[1], pair_recv.at[1], "mp", 1 - mp)
+    copy = remote(sq_mine, sq_other, pair_send.at[1], pair_recv.at[1], "mp", 1 - mp)
+    copy.start()
     copy.wait()
     squares = sq_mine[...] + sq_other[...]
     rate = (clip_bound / jnp.maximum(jnp.sqrt(squares), clip_bound))[0:1, 0:1]
@@ -234,89 +290,99 @@
         )
         return part_a, part_b
 
-    order = target_order(depth)
-    for target in order:
+    far = reduce_order(depth)
+    targets = [pick(far, step, z) for step in range(depth)]
+
+    def sums(src, dst, send_sem, recv_sem, target, cut, index):
+        size = rank // REDUCE_CUTS
+        rows = pl.ds(cut * size, size)
+        return remote(
+            src.at[target, rows], dst.at[target, rows],
+            send_sem.at[target, cut], recv_sem.at[target, cut], "dp", index,
+        )
+
+    def over(target, cut):
+        return sums(cross_out, cross_in, cross_send, cross_recv, target, cut, across)
+
+    def upward(target, cut):
+        return sums(held, up_in, up_send, up_recv, target, cut, above)
+
+    def downward(target, cut):
+        return sums(held, down_in, down_send, down_recv, target, cut, below)
+
+    def add(target, cut, arriving):
+        size = rank // REDUCE_CUTS
+        rows = pl.ds(cut * size, size)
+        held[target, rows] = held[target, rows] + arriving[target, rows]
+
+    for target in targets:
         part_a, part_b = piece(target, other_x)
         cross_out[target, :, :wa] = part_a
         cross_out[target, :, wa:] = part_b
-        copies.append(
-            send(
-                cross_out.at[target], cross_in.at[target],
-                cross_send.at[target], cross_recv.at[target], "dp", across,
-            )
-        )
-    for target in order:
+        for cut in range(REDUCE_CUTS):
+            over(target, cut).start()
+    for target in targets:
         part_a, part_b = piece(target, x)
         held[target, :, :wa] = part_a
         held[target, :, wa:] = part_b
 
-    above = dp + INNER
-    below = dp - INNER
-
-    def from_below(target):
-        arrived(up_in.at[target], up_send.at[target], up_recv.at[target], "dp", dp)
-        held[target] = held[target] + up_in[target]
-
-    def from_above(target):
-        arrived(down_in.at[target], down_send.at[target], down_recv.at[target], "dp", dp)
-        held[target] = held[target] + down_in[target]
-
-    for target in order:
-        arrived(cross_in.at[target], cross_send.at[target], cross_recv.at[target], "dp", across)
-        held[target] = held[target] + cross_in[target]
-
-        @pl.when(z < target)
-        def _():
-            @pl.when(z > 0)
+    for target in targets[:-1]:
+        for cut in range(REDUCE_CUTS):
+            over(target, cut).wait_recv()
+            add(target, cut, cross_in)
+
+            @pl.when(z < target)
             def _():
-                from_below(target)
-
-            send(held.at[target], up_in.at[target], up_send.at[target], up_recv.at[target], "dp", above)
-
-        @pl.when(z > target)
-        def _():
-            @pl.when(z < depth - 1)
+                @pl.when(has_below)
+                def _():
+                    upward(target, cut).wait_recv()
+                    add(target, cut, up_in)
+
+                upward(target, cut).start()
+
+            @pl.when(z > target)
             def _():
-                from_above(target)
-
-            send(
-                held.at[target], down_in.at[target],
-                down_send.at[target], down_recv.at[target], "dp", below,
-            )
+                @pl.when(has_above)
+                def _():
+                    downward(target, cut).wait_recv()
+                    add(target, cut, down_in)
+
+                downward(target, cut).start()
 
     load_na.wait()
     load_nb.wait()
     scale = noise_ratio * clip_bound
-    for target in range(depth):
-
-        @pl.when(z == target)
+    for cut in range(REDUCE_CUTS):
+        over(z, cut).wait_recv()
+        add(z, cut, cross_in)
+
+        @pl.when(has_below)
         def _():
-            if target > 0:
-                from_below(target)
-            if target < depth - 1:
-                from_above(target)
-            out_a_ref[0] = (held[target, :, :wa] + scale * noise_a[...]) / examples
-            out_b_ref[0] = (held[target, :, wa:] + scale * noise_b[...]) / examples
-
-    for copy in copies:
-        copy.wait_send()
-    for target in range(depth):
-
-        @pl.when(z < target)
+            upward(z, cut).wait_recv()
+            add(z, cut, up_in)
+
+        @pl.when(has_above)
         def _():
-            pltpu.make_async_remote_copy(
-                src_ref=held.at[target], dst_ref=up_in.at[target],
-                send_sem=up_send.at[target], recv_sem=up_recv.at[target],
-                device_id={"dp": above}, device_id_type=pl.DeviceIdType.MESH,
-            ).wait_send()
-
-        @pl.when(z > target)
-        def _():
-            pltpu.make_async_remote_copy(
-                src_ref=held.at[target], dst_ref=down_in.at[target],
-                send_sem=down_send.at[target], recv_sem=down_recv.at[target],
-                device_id={"dp": below}, device_id_type=pl.DeviceIdType.MESH,
-            ).wait_send()
+            downward(z, cut).wait_recv()
+            add(z, cut, down_in)
+
+    out_a_ref[0] = (held[z, :, :wa] + scale * noise_a[...]) / examples
+    out_b_ref[0] = (held[z, :, wa:] + scale * noise_b[...]) / examples
+
+    for row in [z] + rows_of:
+        for part in parts:
+            pass_on(part, row, finish)
+    for target in targets:
+        for cut in range(REDUCE_CUTS):
+            over(target, cut).wait_send()
+
+            @pl.when(z < target)
+            def _():
+                upward(target, cut).wait_send()
+
+            @pl.when(z > target)
+            def _():
+                downward(target, cut).wait_send()
 
 
 def fused(depth, inputs, rows, down, up, noise_a, noise_b):
@@ -331,7 +397,7 @@
             jax.ShapeDtypeStruct(noise_a.shape, f32),
             jax.ShapeDtypeStruct(noise_b.shape, f32),
         ),
-        in_specs=[pl.BlockSpec(memory_space=pl.ANY)] * 6,
+        in_specs=[pl.BlockSpec(memory_space=pltpu.HBM)] * 6,
         out_specs=(pl.BlockSpec(memory_space=pltpu.VMEM), pl.BlockSpec(memory_space=pltpu.VMEM)),
         scratch_shapes=[
             pltpu.VMEM(inputs.shape, bf16),
@@ -350,16 +416,16 @@
             pltpu.VMEM((depth, rank, wa + wb), f32),
             pltpu.VMEM((depth, rank, wa + wb), f32),
             dma((6,)),
-            dma((2, 2 * depth)),
-            dma((2, dp)),
+            dma((3, 2, GATHER_CUTS, depth)),
+            dma((2, GATHER_CUTS, dp)),
             dma((2,)),
             dma((2,)),
-            dma((depth,)),
-            dma((depth,)),
-            dma((depth,)),
-            dma((depth,)),
-            dma((depth,)),
-            dma((depth,)),
+            dma((depth, REDUCE_CUTS)),
+            dma((depth, REDUCE_CUTS)),
+            dma((depth, REDUCE_CUTS)),
+            dma((depth, REDUCE_CUTS)),
+            dma((depth, REDUCE_CUTS)),
+            dma((depth, REDUCE_CUTS)),
         ],
         compiler_params=pltpu.CompilerParams(
             collective_id=0, has_side_effects=True, vmem_limit_bytes=40 * 1024 * 1024

time: 82.7 us -> 63.9 us (0.77)
  the two profiles are of different devices: /device:TPU:8 before, /device:TPU:0 now
where the time goes in v2:
time: 63.9 us; the launch traced here: 63.6 us
  Pallas kernels  54.9 us (86%)
  local copies, waits for them, and re-layouts  8.01 us (13%)
  between operations  0.65 us (1%)
    pallas_call x1, Pallas kernels, fused(): pl.pallas_call(functools.partial(kernel, depth), out_shape=(jax.ShapeDtyp...  54.9 us
    unnamed x14, local copies, waits for them, and re-layouts  8.01 us

profile of v2, /device:TPU:0, one launch (start us, length us, event | category | flops | bytes accessed | tf_op | source)
XLA Modules:
  0.0 63.6 jit_solution(13395608158615001815)
XLA Ops:
  0.6 0.0 copy-start
  0.6 2.0 %copy-done = bf16[256,7168]{1,0:T(8,128)(2,1)S(1)} copy-done((bf16[256,7168]{1,0:T(8,128)(2,1)S(1)}, bf16[256,7168]{1,0:T(8,128)(2,1)}, u32[]{:S(2)}) %copy-start) | copy-done | bytes 3670040
  2.7 0.0 copy-start.1
  2.7 1.2 %copy-done.1 = bf16[256,2048]{1,0:T(8,128)(2,1)S(1)} copy-done((bf16[256,2048]{1,0:T(8,128)(2,1)S(1)}, bf16[256,2048]{1,0:T(8,128)(2,1)}, u32[]{:S(2)}) %copy-start.1) | copy-done | bytes 1048600
  3.9 0.0 copy-start.2
  3.9 0.9 %copy-done.2 = f32[1,64,896]{2,1,0:T(8,128)S(1)} copy-done((f32[1,64,896]{2,1,0:T(8,128)S(1)}, f32[1,64,896]{2,1,0:T(8,128)}, u32[]{:S(2)}) %copy-start.2) | copy-done | bytes 229400
  4.8 0.0 copy-start.3
  4.8 0.9 %copy-done.3 = bf16[1,64,896]{2,1,0:T(8,128)(2,1)S(1)} copy-done((bf16[1,64,896]{2,1,0:T(8,128)(2,1)S(1)}, bf16[1,64,896]{2,1,0:T(8,128)(2,1)}, u32[]{:S(2)}) %copy-start.3) | copy-done | bytes 114712
  5.7 0.0 copy-start.4
  5.7 0.8 %copy-done.4 = f32[1,64,256]{2,1,0:T(8,128)S(1)} copy-done((f32[1,64,256]{2,1,0:T(8,128)S(1)}, f32[1,64,256]{2,1,0:T(8,128)}, u32[]{:S(2)}) %copy-start.4) | copy-done | bytes 65560
  6.6 0.0 copy-start.5
  6.6 0.8 %copy-done.5 = bf16[1,64,256]{2,1,0:T(8,128)(2,1)S(1)} copy-done((bf16[1,64,256]{2,1,0:T(8,128)(2,1)S(1)}, bf16[1,64,256]{2,1,0:T(8,128)(2,1)}, u32[]{:S(2)}) %copy-start.5) | copy-done | bytes 32792
  7.3 54.9 %shard_map.77 = (f32[1,64,256]{2,1,0:T(8,128)S(1)}, f32[1,64,896]{2,1,0:T(8,128)S(1)}) custom-call(bf16[256,2048]{1,0:T(8,128)(2,1)S(1)} %copy-done.1, bf16[256,7168]{1,0:T(8,128)(2,1)S(1)} %copy-done, bf16[1,64,256]{2,1,0:T(8,128)(2,1)S(1)} %copy-done.5, bf16[1,64,896]{2,1,0:T(8,128)(2,1)S(1)} %copy-done.3, f32[1,64,256]{2,1,0:T(8,128)S(1)} %copy-done.4, ...), custom_call_target="tpu_custom_call" | custom-call | flops 905969664 | bytes 4718592 | tf_op jit(solution)/shard_map/pallas_call | solution.py:394
  62.3 0.6 copy.10
  62.9 0.7 %copy.11 = f32[1,64,896]{2,1,0:T(8,128)} copy(f32[1,64,896]{2,1,0:T(8,128)S(1)} %get-tuple-element.5) | data formatting | bytes 458752
Async XLA Ops:
  0.6 2.0 %copy-start = (bf16[256,7168]{1,0:T(8,128)(2,1)S(1)}, bf16[256,7168]{1,0:T(8,128)(2,1)}, u32[]{:S(2)}) copy-start(bf16[256,7168]{1,0:T(8,128)(2,1)} %g_ref.1) | copy-start | bytes 11010052
  2.7 1.2 %copy-start.1 = (bf16[256,2048]{1,0:T(8,128)(2,1)S(1)}, bf16[256,2048]{1,0:T(8,128)(2,1)}, u32[]{:S(2)}) copy-start(bf16[256,2048]{1,0:T(8,128)(2,1)} %x_ref.1) | copy-start | bytes 3145732
  3.9 0.9 %copy-start.2 = (f32[1,64,896]{2,1,0:T(8,128)S(1)}, f32[1,64,896]{2,1,0:T(8,128)}, u32[]{:S(2)}) copy-start(f32[1,64,896]{2,1,0:T(8,128)} %noise_b_ref.1) | copy-start | bytes 688132
  4.8 0.9 %copy-start.3 = (bf16[1,64,896]{2,1,0:T(8,128)(2,1)S(1)}, bf16[1,64,896]{2,1,0:T(8,128)(2,1)}, u32[]{:S(2)}) copy-start(bf16[1,64,896]{2,1,0:T(8,128)(2,1)} %b_ref.1) | copy-start | bytes 344068
  5.7 0.8 %copy-start.4 = (f32[1,64,256]{2,1,0:T(8,128)S(1)}, f32[1,64,256]{2,1,0:T(8,128)}, u32[]{:S(2)}) copy-start(f32[1,64,256]{2,1,0:T(8,128)} %noise_a_ref.1) | copy-start | bytes 196612
  6.6 0.8 %copy-start.5 = (bf16[1,64,256]{2,1,0:T(8,128)(2,1)S(1)}, bf16[1,64,256]{2,1,0:T(8,128)(2,1)}, u32[]{:S(2)}) copy-start(bf16[1,64,256]{2,1,0:T(8,128)(2,1)} %a_ref.1) | copy-start | bytes 98308

commit v3 on v2

--- a/solution.py
+++ b/solution.py
@@ -394,8 +394,8 @@
     return pl.pallas_call(
         functools.partial(kernel, depth),
         out_shape=(
-            jax.ShapeDtypeStruct(noise_a.shape, f32),
-            jax.ShapeDtypeStruct(noise_b.shape, f32),
+            pltpu.VMEM(noise_a.shape, f32),
+            pltpu.VMEM(noise_b.shape, f32),
         ),
         in_specs=[pl.BlockSpec(memory_space=pltpu.HBM)] * 6,
         out_specs=(pl.BlockSpec(memory_space=pltpu.VMEM), pl.BlockSpec(memory_space=pltpu.VMEM)),
@@ -428,7 +428,7 @@
             dma((depth, REDUCE_CUTS)),
         ],
         compiler_params=pltpu.CompilerParams(
-            collective_id=0, has_side_effects=True, vmem_limit_bytes=40 * 1024 * 1024
+            collective_id=0, has_side_effects=True, vmem_limit_bytes=56 * 1024 * 1024
         ),
         cost_estimate=pl.CostEstimate(
             flops=6 * rank * SEQ * dp * (wa + wb),

time: 63.9 us -> 56.2 us (0.88)
  local copies, waits for them, and re-layouts: 8.01 us -> 1.32 us
  Pallas kernels: 54.9 us -> 54.1 us
    unnamed x14 -> x2, local copies, waits for them, and re-layouts: 8.01 us -> 1.32 us
    pallas_call x1, Pallas kernels: 54.9 us -> 54.1 us  [fused(): pl.pallas_call(functools.partial(kernel, depth), out_shape=(pltpu.VMEM(no...]
where the time goes in v3:
time: 56.2 us; the launch traced here: 56.1 us
  Pallas kernels  54.1 us (96%)
  local copies, waits for them, and re-layouts  1.32 us (2%)
  between operations  0.64 us (1%)
    pallas_call x1, Pallas kernels, fused(): pl.pallas_call(functools.partial(kernel, depth), out_shape=(pltpu.VMEM(no...  54.1 us
    unnamed x2, local copies, waits for them, and re-layouts  1.32 us

profile of v3, /device:TPU:0, one launch (start us, length us, event | category | flops | bytes accessed | tf_op | source)
XLA Modules:
  0.0 56.1 jit_solution(12664844977859717575)
XLA Ops:
  0.6 54.1 %shard_map.77 = (f32[1,64,256]{2,1,0:T(8,128)S(1)}, f32[1,64,896]{2,1,0:T(8,128)S(1)}) custom-call(bf16[256,2048]{1,0:T(8,128)(2,1)} %x_ref.1, bf16[256,7168]{1,0:T(8,128)(2,1)} %g_ref.1, bf16[1,64,256]{2,1,0:T(8,128)(2,1)} %a_ref.1, bf16[1,64,896]{2,1,0:T(8,128)(2,1)} %b_ref.1, f32[1,64,256]{2,1,0:T(8,128)} %noise_a_ref.1, f32[1,64,896]{2,1,0:T(8,128)} %noise_b_ref.1), custom_call_target="tpu_custom_call" | custom-call | flops 905969664 | bytes 4718592 | tf_op jit(solution)/shard_map/pallas_call | solution.py:394
  54.7 0.6 %copy.10 = f32[1,64,256]{2,1,0:T(8,128)} copy(f32[1,64,256]{2,1,0:T(8,128)S(1)} %get-tuple-element.2) | data formatting | bytes 131072
  55.4 0.7 %copy.11 = f32[1,64,896]{2,1,0:T(8,128)} copy(f32[1,64,896]{2,1,0:T(8,128)S(1)} %get-tuple-element.3) | data formatting | bytes 458752

commit v4 on v3

--- a/solution.py
+++ b/solution.py
@@ -235,16 +235,15 @@
         more = project(slot)
         return u + more[0], v + more[1]
 
-    last = z
     for row in rows_of:
         for part in parts:
             take(part, row * INNER + x)
             pass_on(part, row, start)
+    for row in rows_of:
         more = project(row * INNER + x)
         u, v = u + more[0], v + more[1]
-        u, v = take_across(last, u, v)
-        last = row
-    u, v = take_across(last, u, v)
+    for row in [z] + rows_of:
+        u, v = take_across(row, u, v)
 
     uv_mine[0] = u
     uv_mine[1] = v

time: 56.2 us -> 54.9 us (0.977)
  Pallas kernels: 54.1 us -> 52.8 us
    pallas_call x1, Pallas kernels: 54.1 us -> 52.8 us  [fused(): pl.pallas_call(functools.partial(kernel, depth), out_shape=(pltpu.VMEM(no...]
where the time goes in v4:
time: 54.9 us; the launch traced here: 54.8 us
  Pallas kernels  52.8 us (96%)
  local copies, waits for them, and re-layouts  1.32 us (2%)
  between operations  0.64 us (1%)
    pallas_call x1, Pallas kernels, fused(): pl.pallas_call(functools.partial(kernel, depth), out_shape=(pltpu.VMEM(no...  52.8 us
    unnamed x2, local copies, waits for them, and re-layouts  1.32 us

profile of v4, /device:TPU:0, one launch (start us, length us, event | category | flops | bytes accessed | tf_op | source)
XLA Modules:
  0.0 54.8 jit_solution(15048851597005398530)
XLA Ops:
  0.6 52.8 %shard_map.77 = (f32[1,64,256]{2,1,0:T(8,128)S(1)}, f32[1,64,896]{2,1,0:T(8,128)S(1)}) custom-call(bf16[256,2048]{1,0:T(8,128)(2,1)} %x_ref.1, bf16[256,7168]{1,0:T(8,128)(2,1)} %g_ref.1, bf16[1,64,256]{2,1,0:T(8,128)(2,1)} %a_ref.1, bf16[1,64,896]{2,1,0:T(8,128)(2,1)} %b_ref.1, f32[1,64,256]{2,1,0:T(8,128)} %noise_a_ref.1, f32[1,64,896]{2,1,0:T(8,128)} %noise_b_ref.1), custom_call_target="tpu_custom_call" | custom-call | flops 905969664 | bytes 4718592 | tf_op jit(solution)/shard_map/pallas_call | solution.py:393
  53.4 0.6 %copy.10 = f32[1,64,256]{2,1,0:T(8,128)} copy(f32[1,64,256]{2,1,0:T(8,128)S(1)} %get-tuple-element.2) | data formatting | bytes 131072
  54.1 0.7 %copy.11 = f32[1,64,896]{2,1,0:T(8,128)} copy(f32[1,64,896]{2,1,0:T(8,128)S(1)} %get-tuple-element.3) | data formatting | bytes 458752

commit v5 on v4

--- a/solution.py
+++ b/solution.py
@@ -224,9 +224,6 @@
         pass_on(part, z, start)
     near = gather_order(depth)
     rows_of = [pick(near, step, z) for step in range(depth - 1)]
-    load_x.wait()
-    load_g.wait()
-    u, v = project(dp)
 
     def take_across(row, u, v):
         slot = row * INNER + other_x
@@ -239,6 +236,9 @@
         for part in parts:
             take(part, row * INNER + x)
             pass_on(part, row, start)
+    load_x.wait()
+    load_g.wait()
+    u, v = project(dp)
     for row in rows_of:
         more = project(row * INNER + x)
         u, v = u + more[0], v + more[1]

time: 54.9 us -> 54.9 us (level)
  no operation moved by 1% of the time
where the time goes in v5:
time: 54.9 us; the launch traced here: 54.8 us
  Pallas kernels  52.8 us (96%)
  local copies, waits for them, and re-layouts  1.32 us (2%)
  between operations  0.64 us (1%)
    pallas_call x1, Pallas kernels, fused(): pl.pallas_call(functools.partial(kernel, depth), out_shape=(pltpu.VMEM(no...  52.8 us
    unnamed x2, local copies, waits for them, and re-layouts  1.32 us

profile of v5, /device:TPU:0, one launch (start us, length us, event | category | flops | bytes accessed | tf_op | source)
XLA Modules:
  0.0 54.8 jit_solution(4882854830966913826)
XLA Ops:
  0.6 52.8 %shard_map.77 = (f32[1,64,256]{2,1,0:T(8,128)S(1)}, f32[1,64,896]{2,1,0:T(8,128)S(1)}) custom-call(bf16[256,2048]{1,0:T(8,128)(2,1)} %x_ref.1, bf16[256,7168]{1,0:T(8,128)(2,1)} %g_ref.1, bf16[1,64,256]{2,1,0:T(8,128)(2,1)} %a_ref.1, bf16[1,64,896]{2,1,0:T(8,128)(2,1)} %b_ref.1, f32[1,64,256]{2,1,0:T(8,128)} %noise_a_ref.1, f32[1,64,896]{2,1,0:T(8,128)} %noise_b_ref.1), custom_call_target="tpu_custom_call" | custom-call | flops 905969664 | bytes 4718592 | tf_op jit(solution)/shard_map/pallas_call | solution.py:393
  53.4 0.6 %copy.10 = f32[1,64,256]{2,1,0:T(8,128)} copy(f32[1,64,256]{2,1,0:T(8,128)S(1)} %get-tuple-element.2) | data formatting | bytes 131072
  54.1 0.7 %copy.11 = f32[1,64,896]{2,1,0:T(8,128)} copy(f32[1,64,896]{2,1,0:T(8,128)S(1)} %get-tuple-element.3) | data formatting | bytes 458752
